TPU v7x, 256 devices: a whole 4x4x8 slice. The times are simulated.
256 devices in a mesh: row: 16 (over y, z_hi), col: 16 (over x, z_lo, core).
Axes of the slice: x: 4, y: 4, z: 8 (z_hi: 4, z_lo: 2; z = z_hi * 2 + z_lo), core: 2. Of those that a mesh axis runs over, the one named last changes fastest.
Arguments:
- tokens: bfloat16 [4096, 3072], P('row', 'col'), may hold values from -6 to 6
- out_grad: bfloat16 [4096, 3072], P('row', 'col'), may hold values from -12 to 12
- w_up: bfloat16 [3072, 12288], P('row', 'col'), may hold values from -0.109375 to 0.109375
- w_down: bfloat16 [3072, 12288], P('row', 'col'), may hold values from -0.109375 to 0.109375
Outputs:
- input_grad: bfloat16 [4096, 3072], P('row', 'col')
- up_grad: float32 [3072, 12288], P('row', 'col')
- down_grad: float32 [3072, 12288], P('row', 'col')
All inputs are finite; a program needn't handle non-finite values.
Results may differ from a plain program's by a relative error of at most 0.0049.
Values may be sent and summed in bfloat16 or wider, within the bound.
A program may use at most 128 MiB of HBM per device.

v0:
```python
import math

import jax
import jax.numpy as jnp
from jax import lax
from jax.sharding import PartitionSpec as P

gelu_coef = math.sqrt(2.0 / math.pi)
cubic_coef = 0.044715


def gelu_pair(hidden):
    inner = gelu_coef * (hidden + cubic_coef * hidden * hidden * hidden)
    tangent = jnp.tanh(inner)
    active = 0.5 * hidden * (1.0 + tangent)
    slope = 0.5 * (1.0 + tangent) + 0.5 * hidden * (1.0 - tangent * tangent) * gelu_coef * (
        1.0 + 3.0 * cubic_coef * hidden * hidden
    )
    return (active, slope)


def outer_rows(left, right):
    return lax.dot_general(
        left, right, (((0,), (0,)), ((), ())), preferred_element_type=jnp.float32
    )


def body(tokens, out_grad, w_up, w_down):
    tok_rows, grad_rows = (
        lax.all_gather(tokens, "col", axis=1, tiled=True),
        lax.all_gather(out_grad, "col", axis=1, tiled=True),
    )
    row_count = tok_rows.shape[0]
    factor = 1.0 / math.sqrt(row_count * lax.axis_size("row"))
    tok_cols = tok_rows
    grad_cols = grad_rows
    first = jnp.dot(
        tok_cols,
        lax.all_gather(w_up, "row", axis=0, tiled=True),
        preferred_element_type=jnp.float32,
    )
    second = jnp.dot(
        grad_cols,
        lax.all_gather(w_down, "row", axis=0, tiled=True),
        preferred_element_type=jnp.float32,
    )
    active, slope = gelu_pair(first)
    active = active.astype(jnp.bfloat16)
    hidden_grad = (second * slope).astype(jnp.bfloat16)
    partial_input = lax.dot_general(
        hidden_grad,
        lax.all_gather(w_up, "row", axis=0, tiled=True),
        (((1,), (1,)), ((), ())),
        preferred_element_type=jnp.float32,
    )
    input_grad = lax.psum_scatter(partial_input, "col", scatter_dimension=1, tiled=True).astype(
        jnp.bfloat16
    )
    tok_cols = tok_rows
    up_grad = lax.psum_scatter(
        outer_rows(tok_cols, hidden_grad) * factor, "row", scatter_dimension=0, tiled=True
    )
    grad_cols = grad_rows
    down_grad = lax.psum_scatter(
        outer_rows(grad_cols, active) * factor, "row", scatter_dimension=0, tiled=True
    )
    return (input_grad, up_grad, down_grad)


def solution(mesh):
    return jax.shard_map(
        body,
        mesh=mesh,
        in_specs=(P("row", "col"), P("row", "col"), P("row", "col"), P("row", "col")),
        out_specs=(P("row", "col"), P("row", "col"), P("row", "col")),
        check_vma=False,
    )
```

profile of v0, /device:TPU:65, one launch (start us, length us, event | category | flops | bytes accessed | tf_op | source)
XLA Modules:
  0.0 602.8 jit_solution(5218018389136971701)
XLA Ops:
  7.2 0.7 all-gather.9.cloned.1.call-update
  7.9 0.0 all-gather.11.cloned.1.call-start
  7.9 0.7 all-gather.11.cloned.1.call-update
  8.7 0.7 all-gather.5.cloned.1.call-update
  9.4 0.5 all-gather.7.cloned.1.call-update
  10.0 0.0 reduce-scatter.8.cloned.1.call-start
  10.0 38.3 %all-gather.9.cloned.1.call-done = bf16[256,3072]{0,1:T(8,128)(2,1)} async-done(((bf16[256,192]{0,1:T(8,128)(2,1)}), bf16[256,3072]{0,1:T(8,128)(2,1)}) %all-gather.9.cloned.1.call-update) | async-done | bytes 1572880 | tf_op jit(solution)/shard_map/all_gather | solution.py:30
  48.3 84.5 %all-gather.11.cloned.1.call-done = bf16[3072,768]{1,0:T(8,128)(2,1)} async-done(((bf16[192,768]{1,0:T(8,128)(2,1)}), bf16[3072,768]{1,0:T(8,128)(2,1)}) %all-gather.11.cloned.1.call-update) | async-done | bytes 4718608 | tf_op jit(solution)/shard_map/all_gather | solution.py:39
  132.8 4.2 fusion.14
  137.0 32.2 %all-gather.5.cloned.1.call-done = bf16[256,3072]{0,1:T(8,128)(2,1)} async-done(((bf16[256,192]{0,1:T(8,128)(2,1)}), bf16[256,3072]{0,1:T(8,128)(2,1)}) %all-gather.5.cloned.1.call-update) | async-done | bytes 1572880 | tf_op jit(solution)/shard_map/all_gather | solution.py:31
  169.3 84.4 %all-gather.7.cloned.1.call-done = bf16[3072,768]{1,0:T(8,128)(2,1)} async-done(((bf16[192,768]{1,0:T(8,128)(2,1)}), bf16[3072,768]{1,0:T(8,128)(2,1)}) %all-gather.7.cloned.1.call-update) | async-done | bytes 4718608 | tf_op jit(solution)/shard_map/all_gather | solution.py:44
  253.6 4.7 fusion
  258.3 3.2 fusion.15
  261.5 0.0 reduce-scatter.12.cloned.1.call-start
  261.6 5.2 multiply_bitcast_fusion
  266.8 9.7 %copy.13 = f32[3072,768]{1,0:T(8,128)} copy(f32[3072,768]{0,1:T(8,128)} %multiply_bitcast_fusion) | data formatting | bytes 18874368
  276.5 0.0 reduce-scatter.10.cloned.1.call-start
  276.5 1.3 copy-done.1
  277.9 5.1 multiply_bitcast_fusion.1
  283.0 9.6 %copy.11 = f32[3072,768]{1,0:T(8,128)} copy(f32[3072,768]{0,1:T(8,128)} %multiply_bitcast_fusion.1) | data formatting | bytes 18874368
  292.7 34.2 %reduce-scatter.8.cloned.1.call-done = f32[256,192]{0,1:T(8,128)} async-done(((f32[256,3072]{0,1:T(8,128)}), f32[256,192]{0,1:T(8,128)}) %reduce-scatter.8.cloned.1.call-update) | async-done | bytes 196624 | tf_op jit(solution)/shard_map/reduce_scatter | solution.py:56
  326.9 1.6 convert_element_type.10
  328.5 134.5 %reduce-scatter.12.cloned.1.call-done = f32[192,768]{1,0:T(8,128)} async-done(((f32[3072,768]{1,0:T(8,128)}), f32[192,768]{1,0:T(8,128)}) %reduce-scatter.12.cloned.1.call-update) | async-done | bytes 589840
  463.0 132.9 %reduce-scatter.10.cloned.1.call-done = f32[192,768]{1,0:T(8,128)} async-done(((f32[3072,768]{1,0:T(8,128)}), f32[192,768]{1,0:T(8,128)}) %reduce-scatter.10.cloned.1.call-update) | async-done | bytes 589840
  (11 shorter events, 0.2 us)
Async XLA Ops:
  7.2 41.1 %all-gather.9.cloned.1.call-start = ((), (), s32[]{:S(2)}) async-start(), calls=%async_computation.5 | async-start | bytes 1671168 | tf_op jit(solution)/shard_map/all_gather | solution.py:30
  7.9 124.9 %all-gather.11.cloned.1.call-start = ((), (), s32[]{:S(2)}) async-start(), calls=%async_computation.6 | async-start | bytes 5013504 | tf_op jit(solution)/shard_map/all_gather | solution.py:39
  8.6 160.6 %all-gather.5.cloned.1.call-start = ((), (), s32[]{:S(2)}) async-start(), calls=%async_computation.3 | async-start | bytes 1671168 | tf_op jit(solution)/shard_map/all_gather | solution.py:31
  9.4 244.2 %all-gather.7.cloned.1.call-start = ((), (), s32[]{:S(2)}) async-start(), calls=%async_computation.4 | async-start | bytes 5013504 | tf_op jit(solution)/shard_map/all_gather | solution.py:44
  10.0 316.9 %reduce-scatter.8.cloned.1.call-start = ((), (), s32[]{:S(2)}) async-start(), calls=%async_computation.7 | async-start | bytes 3342336 | tf_op jit(solution)/shard_map/reduce_scatter | solution.py:56
  253.6 4.7 copy-start
  258.3 3.3 copy-start.2
  261.5 201.5 %reduce-scatter.12.cloned.1.call-start = ((), (), s32[]{:S(2)}) async-start(), calls=%async_computation.9 | async-start | bytes 10027008
  276.5 1.4 copy-start.1
  276.5 319.5 %reduce-scatter.10.cloned.1.call-start = ((), (), s32[]{:S(2)}) async-start(), calls=%async_computation.8 | async-start | bytes 10027008
Sparse Core Ops, SparseCore 0:
  9.8 38.3 all-gather.8
  50.7 81.9 all-gather.10
  134.6 34.5 all-gather.4
  171.6 81.9 all-gather.6
  261.6 65.1 reduce-scatter.7
  331.1 131.8 reduce-scatter.11
  467.8 128.0 reduce-scatter.9
where the time goes:
time: 605 us; the launch traced here: 603 us
  waiting for transfers between devices  544 us (90%)
  matrix products  22.5 us (4%)
  local copies, waits for them, and re-layouts  20.6 us (3%)
  between operations  14.2 us (2%)
    unnamed x9, waiting for transfers between devices  270 us
    all_gather x1, waiting for transfers between devices, body(): lax.all_gather(w_up, 'row', axis=0, tiled=True)  84.5 us
    all_gather x1, waiting for transfers between devices, body(): lax.all_gather(w_down, 'row', axis=0, tiled=True)  84.4 us
    all_gather x1, waiting for transfers between devices, body(): lax.all_gather(tokens, 'col', axis=1, tiled=True)  38.3 us
    reduce_scatter x1, waiting for transfers between devices, body(): lax.psum_scatter(partial_input, 'col', scatter_dimension=1, tiled=True)  34.2 us
    all_gather x1, waiting for transfers between devices, body(): lax.all_gather(out_grad, 'col', axis=1, tiled=True)  32.2 us
    unnamed x8, local copies, waits for them, and re-layouts  20.6 us
  transfers between devices with their start and end apart: 7, of which 7 were waited for; matrix products, arithmetic and copies ran while one was open for 6% of the time, Pallas kernels for 0%

commit v1 on v0

v1 whole, which is shorter than its diff:
```python
import math

import jax
import jax.numpy as jnp
from jax import lax
from jax.experimental import pallas as pl
from jax.experimental.pallas import tpu as pltpu
from jax.sharding import PartitionSpec as P

gelu_coef = math.sqrt(2.0 / math.pi)
cubic_coef = 0.044715
MESH = pl.DeviceIdType.MESH
BF16 = jnp.bfloat16
F32 = jnp.float32


def gelu_pair(hidden):
    inner = gelu_coef * (hidden + cubic_coef * hidden * hidden * hidden)
    tangent = jnp.tanh(inner)
    active = 0.5 * hidden * (1.0 + tangent)
    slope = 0.5 * (1.0 + tangent) + 0.5 * hidden * (1.0 - tangent * tangent) * gelu_coef * (
        1.0 + 3.0 * cubic_coef * hidden * hidden
    )
    return (active, slope)


class Slots:
    def __init__(self):
        self.at = {}
        self.count = 0

    def __call__(self, key, extent=1):
        if key not in self.at:
            self.at[key] = self.count
            self.count += extent
        return self.at[key]


SEMS = 256


def kernel(
    tok, og, wu, wd, dw_out, ig_out,
    X, W, H, hb, igs, igr, zs, zr, own_sum, last, ds, dr, dws, dwr, dwl,
    send_sems, recv_sems, local_sems,
):
    row, col = lax.axis_index("row"), lax.axis_index("col")
    x, y = lax.div(col, 4), lax.div(row, 4)
    zh, zl, k = lax.rem(row, 4), lax.rem(lax.div(col, 2), 2), lax.rem(col, 2)
    z = 2 * zh + zl
    o = 1 - k
    mod4 = lambda v: lax.rem(v + 8, 4)
    mod8 = lambda v: lax.rem(v + 16, 8)

    def dev(dx=0, dy=0, zz=None, core=None):
        zz = z if zz is None else zz
        core = k if core is None else core
        xx = mod4(x + dx) if dx else x
        yy = mod4(y + dy) if dy else y
        return (yy * 4 + lax.div(zz, 2), xx * 4 + lax.rem(zz, 2) * 2 + core)

    sib = dev(core=o)
    xp, xm = dev(dx=1), dev(dx=-1)
    yp, ym = dev(dy=1), dev(dy=-1)
    zp, zm = dev(zz=mod8(z + 1)), dev(zz=mod8(z - 1))

    barrier = pltpu.get_barrier_semaphore()
    partners = [sib, xp, xm, yp, ym]
    for rel in range(1, 8):
        for core in (k, o):
            partners.append(dev(zz=mod8(z + rel), core=core))
    for partner in partners:
        pl.semaphore_signal(barrier, inc=1, device_id=partner, device_id_type=MESH)
    pl.semaphore_wait(barrier, len(partners))

    send_no, recv_no, local_no = Slots(), Slots(), Slots()
    sent = []

    def copy_to(src, dst, key, device, recv_at=None):
        recv_at = recv_no(key) if recv_at is None else recv_at
        return pltpu.make_async_remote_copy(
            src_ref=src,
            dst_ref=dst,
            send_sem=send_sems.at[send_no(key)],
            recv_sem=recv_sems.at[recv_at],
            device_id=device,
            device_id_type=MESH,
        )

    def send(src, dst, key, device, recv_at=None):
        copy = copy_to(src, dst, key, device, recv_at)
        copy.start()
        sent.append((None, copy))

    def send_unless(own, src, dst, key, device, recv_at):
        copy = copy_to(src, dst, key, device, recv_at)
        local = pltpu.make_async_copy(src, dst, recv_sems.at[recv_at])

        @pl.when(own)
        def _():
            local.start()

        @pl.when(jnp.logical_not(own))
        def _():
            copy.start()

        sent.append((jnp.logical_not(own), copy))

    def recv(dst, key=None, at=None):
        at = recv_no(key) if at is None else at
        pltpu.make_async_remote_copy(
            src_ref=dst,
            dst_ref=dst,
            send_sem=send_sems.at[0],
            recv_sem=recv_sems.at[at],
            device_id=sib,
            device_id_type=MESH,
        ).wait_recv()

    def w_rows(a, yy, zz):
        return W.at[a, yy, pl.ds(pl.multiple_of(zz * 192, 192), 192), :]

    w_base = recv_no("w", 4)
    for h in range(2):
        for a, src in enumerate((wu, wd)):
            zt = 2 * k + h
            send_unless(
                jnp.logical_and(zt == zh, k == a),
                src.at[:, h * 384 : (h + 1) * 384],
                w_rows(a, y, zh),
                ("w", h, a),
                dev(zz=2 * zt + zl, core=a),
                w_base + zh,
            )

    def shard(a, xx, zz):
        return X.at[
            a, xx,
            pl.ds(pl.multiple_of(lax.rem(zz, 2) * 384, 384), 384),
            pl.ds(pl.multiple_of(lax.div(zz, 2) * 128, 128), 128),
        ]

    def part(a, core):
        return X.at[
            a, x,
            pl.ds(pl.multiple_of(zl * 384 + core * 192, 192), 192),
            pl.ds(pl.multiple_of(zh * 128, 128), 128),
        ]

    mine = pl.ds(pl.multiple_of(k * 128, 128), 128)
    other = pl.ds(pl.multiple_of(o * 128, 128), 128)
    locals_ = []
    for a, src in enumerate((tok, og)):
        send(src.at[:, other], part(a, k), ("half", a), sib)
        copy = pltpu.make_async_copy(src.at[:, mine], part(a, k), local_sems.at[a])
        copy.start()
        locals_.append(copy)
    for a in range(2):
        locals_[a].wait()
        recv(part(a, o), ("half", a))

    steps = [[(0, 0)], [(-1, 1), (1, -1)], [(-2, 1), (2, -1)], [(-3, 1), (3, -1)], [(4, 0)]]

    def arrive(step):
        for a in range(2):
            for rel, way in steps[step]:
                block = shard(a, x, mod8(z + rel))
                if step == 0:
                    send(block, block, ("z", -1, a), zp)
                    send(block, block, ("z", 1, a), zm)
                else:
                    recv(block, ("z", rel, a))
                    if way == 1 and (step < 3 or (step == 3 and a == 0)):
                        send(block, block, ("z", rel - 1 if step < 3 else 4, a), zp)
                    if way == -1 and (step < 3 or (step == 3 and a == 1)):
                        send(block, block, ("z", rel + 1 if step < 3 else 4, a), zm)
                send(block, block, ("x", -1, rel, a), xp)
                send(block, block, ("x", 1, rel, a), xm)

    def across(step):
        for a in range(2):
            for rel, _ in steps[step]:
                zz = mod8(z + rel)
                left, right = shard(a, mod4(x - 1), zz), shard(a, mod4(x + 1), zz)
                recv(left, ("x", -1, rel, a))
                if a == 0:
                    send(left, left, ("x", 2, rel, a), xp)
                recv(right, ("x", 1, rel, a))
                if a == 1:
                    send(right, right, ("x", 2, rel, a), xm)

    order = [0, 1, 3, 2]
    arrive(0)

    for i, off in enumerate(order):
        zz = mod4(zh + off)
        block = w_rows(k, y, zz)
        recv(block, at=w_base + zz)
        send(block, block, ("wy", -1, i), yp)
        send(block, block, ("wy", 1, i), ym)
        send(block, block, ("wk", 0, i), sib)
        if i == 1:
            arrive(1)
    for i, off in enumerate(order):
        zz = mod4(zh + off)
        left, right = w_rows(k, mod4(y - 1), zz), w_rows(k, mod4(y + 1), zz)
        recv(left, ("wy", -1, i))
        if i < 2:
            send(left, left, ("wy", 2, i), yp)
        send(left, left, ("wk", -1, i), sib)
        recv(right, ("wy", 1, i))
        if i >= 2:
            send(right, right, ("wy", 2, i), ym)
        send(right, right, ("wk", 1, i), sib)
        if i == 0:
            across(0)
            arrive(2)
        if i == 2:
            across(1)
            arrive(3)
    across(2)
    arrive(4)
    for i, off in enumerate(order):
        far = w_rows(k, mod4(y + 2), mod4(zh + off))
        recv(far, ("wy", 2, i))
        send(far, far, ("wk", 2, i), sib)
    across(3)
    across(4)
    for rel in (0, -1, 1, 2):
        for i, off in enumerate(order):
            recv(w_rows(o, mod4(y + rel), mod4(zh + off)), ("wk", rel, i))

    for n, rel in enumerate((0, -1, 1, 2)):
        blk = mod4(x + rel)
        if rel == 2:
            for step in range(5):
                for a in range(2):
                    for zrel, _ in steps[step]:
                        recv(shard(a, blk, mod8(z + zrel)), ("x", 2, zrel, a))
        for a in range(2):
            term = lax.dot_general(
                W[a, blk], X[a, blk], (((0,), (0,)), ((), ())), preferred_element_type=F32
            )
            if n == 0:
                H[a] = term
            else:
                H[a] += term

    @pl.loop(0, 6)
    def _(i):
        rows = pl.ds(pl.multiple_of(i * 64, 64), 64)
        active, slope = gelu_pair(H[0, rows, :])
        hb[0, rows, :] = (H[1, rows, :] * slope).astype(BF16)
        hb[1, rows, :] = active.astype(BF16)

    pieces = [(hf, r) for r in range(2) for hf in range(2)]

    def ig_dot(blk, hf, r):
        return jnp.dot(
            W[0, blk, r * 384 : (r + 1) * 384, :],
            hb[0, :, hf * 256 : (hf + 1) * 256],
            preferred_element_type=F32,
        )

    def dw_dot(a, blk, rows):
        return lax.dot_general(
            X[a, blk, rows, :], hb[a], (((1,), (1,)), ((), ())), preferred_element_type=F32
        )

    def ig_send(stage, hf, r, value, device):
        igs[stage, hf, r] = value.astype(BF16)
        send(igs.at[stage, hf, r], igr.at[stage, hf, r], ("ig", stage, hf, r), device)

    def ig_recv(stage, hf, r):
        recv(igr.at[stage, hf, r], ("ig", stage, hf, r))
        return igr[stage, hf, r].astype(F32)

    y_rels = (2, 1, -1, 0)

    def dw_other(n):
        blk = mod4(y + y_rels[n])
        for i in range(2):
            rows = slice(i * 384, (i + 1) * 384)
            ds[n, rows, :] = dw_dot(o, blk, rows).astype(BF16)
            send(ds.at[n, rows, :], dr.at[n, rows, :], ("dk", n, i), sib)

    got = set()

    def dw_own(n, hf, j):
        if (n, hf) not in got:
            rows = slice(hf * 384, (hf + 1) * 384)
            recv(dr.at[n, rows, :], ("dk", n, hf))
            got.add((n, hf))
        rows = slice((2 * hf + j) * 192, (2 * hf + j + 1) * 192)
        return dw_dot(k, mod4(y + y_rels[n]), rows) + dr[n, rows, :].astype(F32)

    def dw_send(stage, hf, j, value, device):
        dws[stage, hf, j] = value.astype(BF16)
        send(dws.at[stage, hf, j], dwr.at[stage, hf, j], ("dw", stage, hf, j), device)

    def dw_recv(stage, hf, j):
        recv(dwr.at[stage, hf, j], ("dw", stage, hf, j))
        return dwr[stage, hf, j].astype(F32)

    for hf, r in pieces:
        ig_send(0, hf, r, ig_dot(mod4(x + 2), hf, r), xm if hf else xp)
    dw_other(0)
    for hf, r in pieces:
        ig_send(1, hf, r, ig_dot(mod4(x + 1 if hf else x - 1), hf, r), xp if hf else xm)
    dw_other(1)
    dw_other(2)
    for hf, j in pieces:
        dw_send(0, hf, j, dw_own(0, hf, j), ym if hf else yp)
    dw_other(3)
    for hf, j in pieces:
        dw_send(1, hf, j, dw_own(1 if hf else 2, hf, j), yp if hf else ym)
    for hf, r in pieces:
        value = ig_dot(mod4(x - 1 if hf else x + 1), hf, r) + ig_recv(0, hf, r)
        ig_send(2, hf, r, value, xm if hf else xp)
    for hf, j in pieces:
        value = dw_own(2 if hf else 1, hf, j) + dw_recv(0, hf, j)
        dw_send(2, hf, j, value, ym if hf else yp)

    z_base = recv_no("zr", 8)
    for hf, r in pieces:
        value = ig_dot(x, hf, r) + ig_recv(1, hf, r) + ig_recv(2, hf, r)
        for j in range(2):
            zt = 2 * (2 * hf + j) + r
            block = value[:, j * 128 : (j + 1) * 128]
            zs[zt] = block.astype(BF16)
            copy = copy_to(zs.at[zt], zr.at[z], ("zs", zt), dev(zz=zt), z_base + z)

            @pl.when(zt == z)
            def _():
                own_sum[...] = block

            @pl.when(zt != z)
            def _():
                copy.start()

            sent.append((zt != z, copy))

    d_base = recv_no("dl", 4)

    def dw_place(a, h):
        return dw_out.at[a, :, pl.ds(pl.multiple_of(h * 384, 128), 384)]

    for hf, j in pieces:
        value = dw_own(3, hf, j) + dw_recv(1, hf, j) + dw_recv(2, hf, j)
        zf = 2 * hf + j
        dwl[zf] = value.astype(BF16)
        half = lax.rem(zh, 2)
        send_unless(
            jnp.logical_and(zf == zh, lax.div(zh, 2) == k),
            dwl.at[zf],
            dw_place(k, half),
            ("dl", zf),
            dev(zz=2 * zf + zl, core=lax.div(zh, 2)),
            d_base + 2 * k + half,
        )

    total = own_sum[...]
    for rel in (1, 7, 2, 6, 3, 5, 4):
        zz = mod8(z + rel)
        recv(zr.at[zz], at=z_base + zz)
        total = total + zr[zz].astype(F32)
    last[...] = total.astype(BF16)
    lanes = pl.ds(pl.multiple_of(k * 128, 128), 128)
    half = lambda core: last.at[pl.ds(pl.multiple_of(core * 192, 192), 192), :]
    send(half(o), ig_out.at[:, lanes], ("last",), sib)
    copy = pltpu.make_async_copy(half(k), ig_out.at[:, lanes], local_sems.at[2])
    copy.start()
    recv(ig_out.at[:, pl.ds(pl.multiple_of(o * 128, 128), 128)], ("last",))
    copy.wait()
    for a in range(2):
        for h in range(2):
            recv(dw_place(a, h), at=d_base + 2 * a + h)
    for cond, copy in sent:
        if cond is None:
            copy.wait_send()
        else:

            @pl.when(cond)
            def _():
                copy.wait_send()

    assert max(send_no.count, recv_no.count) <= SEMS


def body(tokens, out_grad, w_up, w_down):
    any_ = pl.BlockSpec(memory_space=pl.ANY)
    dw, ig = pl.pallas_call(
        kernel,
        out_shape=(
            jax.ShapeDtypeStruct((2, 192, 768), BF16),
            jax.ShapeDtypeStruct((192, 256), BF16),
        ),
        in_specs=[any_] * 4,
        out_specs=(any_, any_),
        scratch_shapes=[
            pltpu.VMEM((2, 4, 768, 512), BF16),
            pltpu.VMEM((2, 4, 768, 384), BF16),
            pltpu.VMEM((2, 384, 512), F32),
            pltpu.VMEM((2, 384, 512), BF16),
            pltpu.VMEM((3, 2, 2, 384, 256), BF16),
            pltpu.VMEM((3, 2, 2, 384, 256), BF16),
            pltpu.VMEM((8, 384, 128), BF16),
            pltpu.VMEM((8, 384, 128), BF16),
            pltpu.VMEM((384, 128), F32),
            pltpu.VMEM((384, 128), BF16),
            pltpu.VMEM((4, 768, 384), BF16),
            pltpu.VMEM((4, 768, 384), BF16),
            pltpu.VMEM((3, 2, 2, 192, 384), BF16),
            pltpu.VMEM((3, 2, 2, 192, 384), BF16),
            pltpu.VMEM((4, 192, 384), BF16),
            pltpu.SemaphoreType.DMA((SEMS,)),
            pltpu.SemaphoreType.DMA((SEMS,)),
            pltpu.SemaphoreType.DMA((4,)),
        ],
        compiler_params=pltpu.CompilerParams(
            collective_id=0, has_side_effects=True, vmem_limit_bytes=58 * 2**20
        ),
        cost_estimate=pl.CostEstimate(
            flops=6 * 10**9, bytes_accessed=4 * 10**6, transcendentals=2 * 10**5
        ),
        name="ffn_backward",
    )(tokens.T, out_grad.T, w_up, w_down)
    factor = 1.0 / math.sqrt(tokens.shape[0] * lax.axis_size("row"))
    grads = dw.astype(F32) * factor
    return (ig.T, grads[0], grads[1])


def solution(mesh):
    return jax.shard_map(
        body,
        mesh=mesh,
        in_specs=(P("row", "col"), P("row", "col"), P("row", "col"), P("row", "col")),
        out_specs=(P("row", "col"), P("row", "col"), P("row", "col")),
        check_vma=False,
    )
```

time: 605 us -> 139 us (0.23)
  waiting for transfers between devices: 544 us -> 0 us
  Pallas kernels: 0 us -> 134 us
  matrix products: 22.5 us -> 0 us
  local copies, waits for them, and re-layouts: 20.6 us -> 1.73 us
  between operations: 14.2 us -> 0.65 us
    unnamed x9 -> x0, waiting for transfers between devices: 270 us -> none
    all_gather x4 -> x0, waiting for transfers between devices: 239 us -> none  [the longest x1 84.5 us: body(): lax.all_gather(w_up, 'row', axis=0, tiled=True)]
    pallas_call x0 -> x1, Pallas kernels: none -> 134 us  [body(): pl.pallas_call(kernel, out_shape=(jax.ShapeDtypeStruct((2, 192, 768), BF1...]
    reduce_scatter x1 -> x0, waiting for transfers between devices: 34.2 us -> none  [body(): lax.psum_scatter(partial_input, 'col', scatter_dimension=1, tiled=True)]
    dot_general x5 -> x0, matrix products: 22.5 us -> none  [the longest x2 10.4 us: outer_rows(): lax.dot_general(left, right, (((0,), (0,)), ((), ())), preferred_element_...]
    unnamed x8 -> x3, local copies, waits for them, and re-layouts: 20.6 us -> 0.64 us
  transfers between devices with their start and end apart: 7 -> 0, of which waited for: 7 -> 0; matrix products, arithmetic and copies ran while one was open for 6% -> 0% of each run, Pallas kernels for 0% -> 0%
where the time goes in v1:
time: 139 us; the launch traced here: 137 us
  Pallas kernels  134 us (96%)
  local copies, waits for them, and re-layouts  1.73 us (1%)
    pallas_call x1, Pallas kernels, body(): pl.pallas_call(kernel, out_shape=(jax.ShapeDtypeStruct((2, 192, 768), BF1...  134 us

profile of v1, /device:TPU:65, one launch (start us, length us, event | category | flops | bytes accessed | tf_op | source)
XLA Modules:
  0.0 137.2 jit_solution(18411182046275558817)
XLA Ops:
  0.6 133.7 %ffn_backward.1 = (bf16[2,192,768]{2,1,0:T(8,128)(2,1)}, bf16[192,256]{1,0:T(8,128)(2,1)}) custom-call(bf16[192,256]{1,0:T(8,128)(2,1)} %bitcast.8, bf16[192,256]{1,0:T(8,128)(2,1)} %bitcast.9, bf16[192,768]{1,0:T(8,128)(2,1)} %wu.1, bf16[192,768]{1,0:T(8,128)(2,1)} %wd.1), custom_call_target="tpu_custom_call" | custom-call | flops 6000000000 | bytes 4000000 | tf_op jit(solution)/shard_map/ffn_backward/pallas_call | solution.py:392
  134.3 1.1 convert_multiply_fusion
  135.5 0.0 copy-start
  135.5 1.1 slice_bitcast_fusion
  136.6 0.0 copy-done
  136.6 0.6 copy.8
Async XLA Ops:
  135.5 1.1 copy-start

commit v2 on v1

--- a/solution.py
+++ b/solution.py
@@ -41,7 +41,7 @@
 
 def kernel(
     tok, og, wu, wd, dw_out, ig_out,
-    X, W, H, hb, igs, igr, zs, zr, own_sum, last, ds, dr, dws, dwr, dwl,
+    X, W, H, hb, igb, igf, igs, igr, zs, zr, own_sum, last, ds, dr, df, dws, dwr, dwl,
     send_sems, recv_sems, local_sems,
 ):
     row, col = lax.axis_index("row"), lax.axis_index("col")
@@ -65,8 +65,8 @@
     zp, zm = dev(zz=mod8(z + 1)), dev(zz=mod8(z - 1))
 
     barrier = pltpu.get_barrier_semaphore()
-    partners = [sib, xp, xm, yp, ym]
-    for rel in range(1, 8):
+    partners = [sib, xp, xm, yp, ym, zp, zm]
+    for rel in (2, 4, 6):
         for core in (k, o):
             partners.append(dev(zz=mod8(z + rel), core=core))
     for partner in partners:
@@ -253,118 +253,198 @@
         hb[0, rows, :] = (H[1, rows, :] * slope).astype(BF16)
         hb[1, rows, :] = active.astype(BF16)
 
-    pieces = [(hf, r) for r in range(2) for hf in range(2)]
-
-    def ig_dot(blk, hf, r):
-        return jnp.dot(
-            W[0, blk, r * 384 : (r + 1) * 384, :],
-            hb[0, :, hf * 256 : (hf + 1) * 256],
+    def rows_of(start, size, align):
+        return pl.ds(pl.multiple_of(start, align), size)
+
+    def ig_block(rel):
+        for i in range(3):
+            rows = slice(i * 256, (i + 1) * 256)
+            value = jnp.dot(W[0, mod4(x + rel), rows, :], hb[0], preferred_element_type=F32)
+            if rel != 0:
+                igb[rel % 4, rows, :] = value.astype(BF16)
+            if rel != 2:
+                igf[rel % 4, rows, :] = value
+
+    def ig_spot(g, t):
+        zt = mod8(z + (4 - g) * (1, -1)[t])
+        whole = 0 < g < 4
+        start = lax.rem(zt, 2) * 384 + (0 if whole else 192 * t)
+        rows = rows_of(start, 384 if whole else 192, 192)
+        return rows, rows_of(lax.div(zt, 2) * 128, 128, 128)
+
+    def height(g):
+        return slice(0, 384 if 0 < g < 4 else 192)
+
+    def ig_s1(g):
+        for t in range(2):
+            send(
+                igb.at[(2, *ig_spot(g, t))], igr.at[0, g, t, height(g)],
+                ("ig", 0, g, t), (xp, xm)[t],
+            )
+
+    def ig_s2(g):
+        for t in range(2):
+            send(
+                igb.at[((3, 1)[t], *ig_spot(g, t))], igr.at[1, g, t, height(g)],
+                ("ig", 1, g, t), (xm, xp)[t],
+            )
+
+    def ig_recv(stage, g, t):
+        recv(igr.at[stage, g, t, height(g)], ("ig", stage, g, t))
+        return igr[stage, g, t, height(g), :].astype(F32)
+
+    def ig_s3(g):
+        for t in range(2):
+            value = igf[((1, 3)[t], *ig_spot(g, t))] + ig_recv(0, g, t)
+            igs[g, t, height(g), :] = value.astype(BF16)
+            send(
+                igs.at[g, t, height(g)], igr.at[2, g, t, height(g)],
+                ("ig", 2, g, t), (xp, xm)[t],
+            )
+
+    def zc_recv(g, t):
+        recv(zr.at[g, t, height(g)], ("zc", g, t))
+        return zr[g, t, height(g), :].astype(F32)
+
+    def ig_s4(g):
+        for t in range(2):
+            value = igf[(0, *ig_spot(g, t))] + ig_recv(1, g, t) + ig_recv(2, g, t)
+            if g == 4:
+                own_sum[192 * t : 192 * (t + 1), :] = value
+                continue
+            if g > 1:
+                value = value + zc_recv(g - 1, t)
+            zs[g, t, height(g), :] = value.astype(BF16)
+            if g == 1:
+                part_rows = slice(192 * t, 192 * (t + 1))
+                summed = value[part_rows] + zc_recv(0, t)
+                zs[g, t, part_rows, :] = summed.astype(BF16)
+            send(
+                zs.at[g, t, height(g)], zr.at[g, t, height(g)],
+                ("zc", g, t), (zp, zm)[t],
+            )
+
+    def dw_block(a, rel, rows):
+        return lax.dot_general(
+            X[a, mod4(y + rel), rows, :], hb[a], (((1,), (1,)), ((), ())),
             preferred_element_type=F32,
         )
 
-    def dw_dot(a, blk, rows):
-        return lax.dot_general(
-            X[a, blk, rows, :], hb[a], (((1,), (1,)), ((), ())), preferred_element_type=F32
-        )
-
-    def ig_send(stage, hf, r, value, device):
-        igs[stage, hf, r] = value.astype(BF16)
-        send(igs.at[stage, hf, r], igr.at[stage, hf, r], ("ig", stage, hf, r), device)
-
-    def ig_recv(stage, hf, r):
-        recv(igr.at[stage, hf, r], ("ig", stage, hf, r))
-        return igr[stage, hf, r].astype(F32)
-
-    y_rels = (2, 1, -1, 0)
-
-    def dw_other(n):
-        blk = mod4(y + y_rels[n])
+    def dw_other(rel):
         for i in range(2):
             rows = slice(i * 384, (i + 1) * 384)
-            ds[n, rows, :] = dw_dot(o, blk, rows).astype(BF16)
-            send(ds.at[n, rows, :], dr.at[n, rows, :], ("dk", n, i), sib)
-
-    got = set()
-
-    def dw_own(n, hf, j):
-        if (n, hf) not in got:
-            rows = slice(hf * 384, (hf + 1) * 384)
-            recv(dr.at[n, rows, :], ("dk", n, hf))
-            got.add((n, hf))
-        rows = slice((2 * hf + j) * 192, (2 * hf + j + 1) * 192)
-        return dw_dot(k, mod4(y + y_rels[n]), rows) + dr[n, rows, :].astype(F32)
-
-    def dw_send(stage, hf, j, value, device):
-        dws[stage, hf, j] = value.astype(BF16)
-        send(dws.at[stage, hf, j], dwr.at[stage, hf, j], ("dw", stage, hf, j), device)
-
-    def dw_recv(stage, hf, j):
-        recv(dwr.at[stage, hf, j], ("dw", stage, hf, j))
-        return dwr[stage, hf, j].astype(F32)
-
-    for hf, r in pieces:
-        ig_send(0, hf, r, ig_dot(mod4(x + 2), hf, r), xm if hf else xp)
+            ds[rel % 4, rows, :] = dw_block(o, rel, rows).astype(BF16)
+            send(ds.at[rel % 4, rows, :], dr.at[rel % 4, rows, :], ("dk", rel, i), sib)
+
+    def dw_own(rel):
+        for i in range(2):
+            rows = slice(i * 384, (i + 1) * 384)
+            df[rel % 4, rows, :] = dw_block(k, rel, rows)
+
+    def dw_sum(rel):
+        for i in range(2):
+            recv(dr.at[rel % 4, i * 384 : (i + 1) * 384, :], ("dk", rel, i))
+
+    def dw_value(rel, q, t):
+        rows = slice(384 * t + 96 * q, 384 * t + 96 * (q + 1))
+        return df[rel % 4, rows, :] + dr[rel % 4, rows, :].astype(F32)
+
+    def dw_send(stage, q, t, value, device):
+        dws[stage, q, t] = value.astype(BF16)
+        send(dws.at[stage, q, t], dwr.at[stage, q, t], ("dw", stage, q, t), device)
+
+    def dw_recv(stage, q, t):
+        recv(dwr.at[stage, q, t], ("dw", stage, q, t))
+        return dwr[stage, q, t].astype(F32)
+
+    def dw_s1(q):
+        for t in range(2):
+            dw_send(0, q, t, dw_value(2, q, t), (yp, ym)[t])
+
+    def dw_s2(q):
+        for t in range(2):
+            dw_send(1, q, t, dw_value((-1, 1)[t], q, t), (ym, yp)[t])
+
+    def dw_s3(q):
+        for t in range(2):
+            dw_send(2, q, t, dw_value((1, -1)[t], q, t) + dw_recv(0, q, t), (yp, ym)[t])
+
+    d_base = recv_no("dl", 8)
+
+    def dw_place(a, h, q):
+        return dw_out.at[
+            a, 96 * (q % 2) : 96 * (q % 2 + 1), pl.ds(pl.multiple_of(h * 384, 128), 384)
+        ]
+
+    def dw_s4(q):
+        for t in range(2):
+            value = dw_value(0, q, t) + dw_recv(1, q, t) + dw_recv(2, q, t)
+            dwl[q, t] = value.astype(BF16)
+            zf = 2 * t + q // 2
+            half = lax.rem(zh, 2)
+            send_unless(
+                jnp.logical_and(zf == zh, lax.div(zh, 2) == k),
+                dwl.at[q, t],
+                dw_place(k, half, q),
+                ("dl", q, t),
+                dev(zz=2 * zf + zl, core=lax.div(zh, 2)),
+                d_base + 2 * (2 * k + half) + q % 2,
+            )
+
+    ig_block(2)
+    ig_s1(0)
+    ig_s1(1)
+    dw_other(2)
+    ig_block(1)
+    ig_block(-1)
+    ig_s2(0)
+    ig_s2(1)
+    dw_own(2)
+    dw_other(1)
+    dw_other(-1)
+    dw_sum(2)
+    dw_s1(0)
+    dw_s1(1)
+    dw_own(1)
+    dw_own(-1)
+    dw_sum(1)
+    dw_sum(-1)
+    dw_s2(0)
+    dw_s2(1)
+    ig_block(0)
     dw_other(0)
-    for hf, r in pieces:
-        ig_send(1, hf, r, ig_dot(mod4(x + 1 if hf else x - 1), hf, r), xp if hf else xm)
-    dw_other(1)
-    dw_other(2)
-    for hf, j in pieces:
-        dw_send(0, hf, j, dw_own(0, hf, j), ym if hf else yp)
-    dw_other(3)
-    for hf, j in pieces:
-        dw_send(1, hf, j, dw_own(1 if hf else 2, hf, j), yp if hf else ym)
-    for hf, r in pieces:
-        value = ig_dot(mod4(x - 1 if hf else x + 1), hf, r) + ig_recv(0, hf, r)
-        ig_send(2, hf, r, value, xm if hf else xp)
-    for hf, j in pieces:
-        value = dw_own(2 if hf else 1, hf, j) + dw_recv(0, hf, j)
-        dw_send(2, hf, j, value, ym if hf else yp)
-
-    z_base = recv_no("zr", 8)
-    for hf, r in pieces:
-        value = ig_dot(x, hf, r) + ig_recv(1, hf, r) + ig_recv(2, hf, r)
-        for j in range(2):
-            zt = 2 * (2 * hf + j) + r
-            block = value[:, j * 128 : (j + 1) * 128]
-            zs[zt] = block.astype(BF16)
-            copy = copy_to(zs.at[zt], zr.at[z], ("zs", zt), dev(zz=zt), z_base + z)
-
-            @pl.when(zt == z)
-            def _():
-                own_sum[...] = block
-
-            @pl.when(zt != z)
-            def _():
-                copy.start()
-
-            sent.append((zt != z, copy))
-
-    d_base = recv_no("dl", 4)
-
-    def dw_place(a, h):
-        return dw_out.at[a, :, pl.ds(pl.multiple_of(h * 384, 128), 384)]
-
-    for hf, j in pieces:
-        value = dw_own(3, hf, j) + dw_recv(1, hf, j) + dw_recv(2, hf, j)
-        zf = 2 * hf + j
-        dwl[zf] = value.astype(BF16)
-        half = lax.rem(zh, 2)
-        send_unless(
-            jnp.logical_and(zf == zh, lax.div(zh, 2) == k),
-            dwl.at[zf],
-            dw_place(k, half),
-            ("dl", zf),
-            dev(zz=2 * zf + zl, core=lax.div(zh, 2)),
-            d_base + 2 * k + half,
-        )
-
-    total = own_sum[...]
-    for rel in (1, 7, 2, 6, 3, 5, 4):
-        zz = mod8(z + rel)
-        recv(zr.at[zz], at=z_base + zz)
-        total = total + zr[zz].astype(F32)
-    last[...] = total.astype(BF16)
+    dw_own(0)
+    dw_sum(0)
+    ig_s3(0)
+    ig_s1(2)
+    ig_s2(2)
+    dw_s3(0)
+    dw_s1(2)
+    dw_s2(2)
+    ig_s3(1)
+    ig_s1(3)
+    ig_s2(3)
+    ig_s4(0)
+    dw_s3(1)
+    dw_s1(3)
+    dw_s2(3)
+    dw_s4(0)
+    ig_s3(2)
+    ig_s1(4)
+    ig_s2(4)
+    ig_s4(1)
+    dw_s3(2)
+    dw_s4(1)
+    ig_s3(3)
+    ig_s4(2)
+    dw_s3(3)
+    dw_s4(2)
+    ig_s3(4)
+    ig_s4(3)
+    dw_s4(3)
+    ig_s4(4)
+
+    last[...] = (own_sum[...] + zc_recv(3, 0) + zc_recv(3, 1)).astype(BF16)
     lanes = pl.ds(pl.multiple_of(k * 128, 128), 128)
     half = lambda core: last.at[pl.ds(pl.multiple_of(core * 192, 192), 192), :]
     send(half(o), ig_out.at[:, lanes], ("last",), sib)
@@ -374,7 +454,8 @@
     copy.wait()
     for a in range(2):
         for h in range(2):
-            recv(dw_place(a, h), at=d_base + 2 * a + h)
+            for q in range(2):
+                recv(dw_place(a, h, q), at=d_base + 2 * (2 * a + h) + q)
     for cond, copy in sent:
         if cond is None:
             copy.wait_send()
@@ -402,17 +483,20 @@
             pltpu.VMEM((2, 4, 768, 384), BF16),
             pltpu.VMEM((2, 384, 512), F32),
             pltpu.VMEM((2, 384, 512), BF16),
-            pltpu.VMEM((3, 2, 2, 384, 256), BF16),
-            pltpu.VMEM((3, 2, 2, 384, 256), BF16),
-            pltpu.VMEM((8, 384, 128), BF16),
-            pltpu.VMEM((8, 384, 128), BF16),
+            pltpu.VMEM((4, 768, 512), BF16),
+            pltpu.VMEM((4, 768, 512), F32),
+            pltpu.VMEM((5, 2, 384, 128), BF16),
+            pltpu.VMEM((3, 5, 2, 384, 128), BF16),
+            pltpu.VMEM((4, 2, 384, 128), BF16),
+            pltpu.VMEM((4, 2, 384, 128), BF16),
             pltpu.VMEM((384, 128), F32),
             pltpu.VMEM((384, 128), BF16),
             pltpu.VMEM((4, 768, 384), BF16),
             pltpu.VMEM((4, 768, 384), BF16),
-            pltpu.VMEM((3, 2, 2, 192, 384), BF16),
-            pltpu.VMEM((3, 2, 2, 192, 384), BF16),
-            pltpu.VMEM((4, 192, 384), BF16),
+            pltpu.VMEM((4, 768, 384), F32),
+            pltpu.VMEM((3, 4, 2, 96, 384), BF16),
+            pltpu.VMEM((3, 4, 2, 96, 384), BF16),
+            pltpu.VMEM((4, 2, 96, 384), BF16),
             pltpu.SemaphoreType.DMA((SEMS,)),
             pltpu.SemaphoreType.DMA((SEMS,)),
             pltpu.SemaphoreType.DMA((4,)),
@@ -426,8 +510,7 @@
         name="ffn_backward",
     )(tokens.T, out_grad.T, w_up, w_down)
     factor = 1.0 / math.sqrt(tokens.shape[0] * lax.axis_size("row"))
-    grads = dw.astype(F32) * factor
-    return (ig.T, grads[0], grads[1])
+    return (ig.T, dw[0].astype(F32) * factor, dw[1].astype(F32) * factor)
 
 
 def solution(mesh):

time: 139 us -> 125 us (0.90); the launches traced: 137 us -> 125 us
  Pallas kernels: 134 us -> 122 us
    pallas_call x1, Pallas kernels: 134 us -> 122 us  [body(): pl.pallas_call(kernel, out_shape=(jax.ShapeDtypeStruct((2, 192, 768), BF1...]
where the time goes in v2:
time: 125 us
  Pallas kernels  122 us (98%)
  other arithmetic  2.17 us (2%)
    pallas_call x1, Pallas kernels, body(): pl.pallas_call(kernel, out_shape=(jax.ShapeDtypeStruct((2, 192, 768), BF1...  122 us

profile of v2, /device:TPU:65, one launch (start us, length us, event | category | flops | bytes accessed | tf_op | source)
XLA Modules:
  0.0 125.0 jit_solution(3705094890523173021)
XLA Ops:
  0.6 121.6 %ffn_backward.1 = (bf16[2,192,768]{2,1,0:T(8,128)(2,1)}, bf16[192,256]{1,0:T(8,128)(2,1)}) custom-call(bf16[192,256]{1,0:T(8,128)(2,1)} %bitcast.8, bf16[192,256]{1,0:T(8,128)(2,1)} %bitcast.9, bf16[192,768]{1,0:T(8,128)(2,1)} %wu.1, bf16[192,768]{1,0:T(8,128)(2,1)} %wd.1), custom_call_target="tpu_custom_call" | custom-call | flops 6000000000 | bytes 4000000 | tf_op jit(solution)/shard_map/ffn_backward/pallas_call | solution.py:473
  122.2 0.0 copy-start
  122.2 2.2 %multiply_bitcast_fusion = (f32[192,768]{1,0:T(8,128)}, f32[192,768]{1,0:T(8,128)}) fusion(bf16[2,192,768]{2,1,0:T(8,128)(2,1)} %get-tuple-element.6), kind=kLoop, calls=%fused_computation | loop fusion | flops 589824 | bytes 1769472 | tf_op jit(solution)/shard_map/mul | solution.py:513
  124.4 0.0 copy-done
  124.4 0.6 copy.8
Async XLA Ops:
  122.2 2.2 %copy-start = (bf16[192,256]{1,0:T(8,128)(2,1)S(1)}, bf16[192,256]{1,0:T(8,128)(2,1)}, u32[]{:S(2)}) copy-start(bf16[192,256]{1,0:T(8,128)(2,1)} %get-tuple-element.5) | copy-start | bytes 294916

commit v3 on v2

v3 whole, which is shorter than its diff:
```python
import math

import jax
import jax.numpy as jnp
from jax import lax
from jax.experimental import pallas as pl
from jax.experimental.pallas import tpu as pltpu
from jax.sharding import PartitionSpec as P

gelu_coef = math.sqrt(2.0 / math.pi)
cubic_coef = 0.044715
MESH = pl.DeviceIdType.MESH
BF16 = jnp.bfloat16
F32 = jnp.float32


def gelu_pair(hidden):
    inner = gelu_coef * (hidden + cubic_coef * hidden * hidden * hidden)
    tangent = jnp.tanh(inner)
    active = 0.5 * hidden * (1.0 + tangent)
    slope = 0.5 * (1.0 + tangent) + 0.5 * hidden * (1.0 - tangent * tangent) * gelu_coef * (
        1.0 + 3.0 * cubic_coef * hidden * hidden
    )
    return (active, slope)


class Slots:
    def __init__(self):
        self.at = {}
        self.count = 0
        self.bytes = {}

    def __call__(self, key, extent=1):
        if key not in self.at:
            self.at[key] = self.count
            self.count += extent
        return self.at[key]

    def add(self, key, size):
        self.bytes[key] = self.bytes.get(key, 0) + size
        return self(key)


SENDS = 13
RECVS = 76
BLOCK = 192 * 384 * 2


def kernel(
    tok, og, wu, wd, dw_out, ig_out,
    X, W, H, hb, igb, igf, igs, igr, zs, zr, own_sum, last, ds, dr, df, dws, dwr, dwl,
    send_sems, recv_sems, local_sems,
):
    row, col = lax.axis_index("row"), lax.axis_index("col")
    x, y = lax.div(col, 4), lax.div(row, 4)
    zh, zl, k = lax.rem(row, 4), lax.rem(lax.div(col, 2), 2), lax.rem(col, 2)
    z = 2 * zh + zl
    o = 1 - k
    mod4 = lambda v: lax.rem(v + 8, 4)
    mod8 = lambda v: lax.rem(v + 16, 8)

    def dev(dx=0, dy=0, zz=None, core=None):
        zz = z if zz is None else zz
        core = k if core is None else core
        xx = mod4(x + dx) if dx else x
        yy = mod4(y + dy) if dy else y
        return (yy * 4 + lax.div(zz, 2), xx * 4 + lax.rem(zz, 2) * 2 + core)

    sib = dev(core=o)
    xp, xm = dev(dx=1), dev(dx=-1)
    yp, ym = dev(dy=1), dev(dy=-1)
    zp, zm = dev(zz=mod8(z + 1)), dev(zz=mod8(z - 1))

    def part(a, core):
        return X.at[
            a, x,
            pl.ds(pl.multiple_of(zl * 384 + core * 192, 192), 192),
            pl.ds(pl.multiple_of(zh * 128, 128), 128),
        ]

    mine = pl.ds(pl.multiple_of(k * 128, 128), 128)
    other = pl.ds(pl.multiple_of(o * 128, 128), 128)
    kept = [
        pltpu.make_async_copy(src.at[:, mine], part(a, k), local_sems.at[a])
        for a, src in enumerate((tok, og))
    ]
    for copy in kept:
        copy.start()

    barrier = pltpu.get_barrier_semaphore()
    partners = [sib, xp, xm, yp, ym, zp, zm]
    for rel in (2, 4, 6):
        for core in (k, o):
            partners.append(dev(zz=mod8(z + rel), core=core))
    for partner in partners:
        pl.semaphore_signal(barrier, inc=1, device_id=partner, device_id_type=MESH)
    pl.semaphore_wait(barrier, len(partners))

    send_no, recv_no = Slots(), Slots()

    def size_of(ref):
        return math.prod(ref.shape) * 2

    def view(size):
        for lead in (1, 2, 3, 4, 6, 8):
            rows, rest = divmod(size, lead * 1024)
            if rest == 0 and rows <= 768 and rows % 16 == 0:
                if lead < 5:
                    return X.at[0, :lead, :rows, :]
                return X.at[:, : lead // 2, :rows, :]
        for rows in range(768, 0, -16):
            for lead in (1, 2, 3, 4):
                if size == lead * rows * 256:
                    return X.at[0, :lead, :rows, :128]
        raise ValueError(size)

    def dummy(size, send_at=0, recv_at=0):
        return pltpu.make_async_remote_copy(
            src_ref=view(size),
            dst_ref=view(size),
            send_sem=send_sems.at[send_at],
            recv_sem=recv_sems.at[recv_at],
            device_id=sib,
            device_id_type=MESH,
        )

    def send(src, dst, group, key, device):
        size = size_of(src)
        pltpu.make_async_remote_copy(
            src_ref=src,
            dst_ref=dst,
            send_sem=send_sems.at[send_no.add(group, size)],
            recv_sem=recv_sems.at[recv_no.add(key, size)],
            device_id=device,
            device_id_type=MESH,
        ).start()

    def send_unless(own, src, dst, group, device, recv_at):
        copy = pltpu.make_async_remote_copy(
            src_ref=src,
            dst_ref=dst,
            send_sem=send_sems.at[send_no(group)],
            recv_sem=recv_sems.at[recv_at],
            device_id=device,
            device_id_type=MESH,
        )
        local = pltpu.make_async_copy(src, dst, recv_sems.at[recv_at])

        @pl.when(own)
        def _():
            local.start()

        @pl.when(jnp.logical_not(own))
        def _():
            copy.start()

    def recv(key):
        dummy(recv_no.bytes[key], recv_at=recv_no(key)).wait_recv()

    def w_rows(a, yy, zz):
        return W.at[a, yy, pl.ds(pl.multiple_of(zz * 192, 192), 192), :]

    w_base = recv_no("w", 4)

    def w_out(a):
        for h in range(2):
            zt = 2 * k + h
            send_unless(
                jnp.logical_and(zt == zh, k == a),
                (wu, wd)[a].at[:, h * 384 : (h + 1) * 384],
                w_rows(a, y, zh),
                "w",
                dev(zz=2 * zt + zl, core=a),
                w_base + zh,
            )

    for a, src in enumerate((tok, og)):
        send(src.at[:, other], part(a, k), "half", "half", sib)
    w_out(0)
    w_out(1)

    def lanes_of(zz):
        return pl.ds(pl.multiple_of(lax.div(zz, 2) * 128, 128), 128)

    def tok_shard(xx, zz):
        start = lax.rem(zz, 2) * 384
        return X.at[0, xx, pl.ds(pl.multiple_of(start, 384), 384), lanes_of(zz)]

    def og_shard(xx, zz):
        start = lax.rem(zz, 2) * 384
        return X.at[1, xx, pl.ds(pl.multiple_of(start, 384), 192), lanes_of(zz)]

    def rest_shard(xx, start, size):
        first = zl * 384 + 192 + start
        return X.at[1, xx, pl.ds(pl.multiple_of(first, 96), size), lanes_of(z)]

    def rest_shards(xs, zz):
        first = lax.rem(zz, 2) * 384 + 192
        return X.at[1, xs, pl.ds(pl.multiple_of(first, 192), 192), lanes_of(zz)]

    steps = [[0], [-1, 1], [-2, 2], [-3, 3], [4]]

    def arrive(step):
        for rel in steps[step]:
            blocks = [tok_shard(x, mod8(z + rel)), og_shard(x, mod8(z + rel))]
            if step > 0:
                recv(("z", rel))
            for n, block in enumerate(blocks):
                if step < 3 and rel <= 0:
                    send(block, block, "z", ("z", rel - 1), zp)
                if step < 3 and rel >= 0:
                    send(block, block, "z", ("z", rel + 1), zm)
                if rel == -3 and n == 0:
                    send(block, block, "z", ("z", 4), zp)
                if rel == 3 and n == 1:
                    send(block, block, "z", ("z", 4), zm)
            for block in blocks:
                send(block, block, "x", ("x", -1, rel), xp)
                send(block, block, "x", ("x", 1, rel), xm)

    def across(step):
        for rel in steps[step]:
            zz = mod8(z + rel)
            shards = (tok_shard, og_shard) if rel % 2 == 0 else (og_shard, tok_shard)
            left, right = shards[0](mod4(x - 1), zz), shards[1](mod4(x + 1), zz)
            recv(("x", -1, rel))
            send(left, left, "x", "far", xp)
            recv(("x", 1, rel))
            send(right, right, "x", "far", xm)

    def rest_x(step):
        if step == 0:
            block = rest_shard(x, 0, 192)
            send(block, block, "rest", "rest near", xp)
            send(block, block, "rest", "rest near", xm)
        if step == 1:
            recv("rest near")
            left, right = rest_shard(mod4(x - 1), 0, 96), rest_shard(mod4(x + 1), 96, 96)
            send(left, left, "rest", "rest far", xp)
            send(right, right, "rest", "rest far", xm)
        if step == 2:
            recv("rest far")

    def rest_z(step):
        for way in (-1, 1):
            if step > 0:
                recv(("rest", way * step))
            if step < 3:
                block = rest_shards(slice(0, 4), mod8(z + way * step))
                send(block, block, "rest", ("rest", way * (step + 1)), zp if way < 0 else zm)
            else:
                xs = slice(0, 2) if way < 0 else slice(2, 4)
                block = rest_shards(xs, mod8(z + way * step))
                send(block, block, "rest", ("rest", 4), zp if way < 0 else zm)

    order = [0, 1, 3, 2]

    def w_in(i):
        zz = mod4(zh + order[i])
        block = w_rows(k, y, zz)
        dummy(BLOCK, recv_at=w_base + zz).wait_recv()
        send(block, block, "wy", ("wy", -1, i), yp)
        send(block, block, "wy", ("wy", 1, i), ym)
        send(block, block, "wk", "wk", sib)

    def w_ring(i):
        zz = mod4(zh + order[i])
        left, right = w_rows(k, mod4(y - 1), zz), w_rows(k, mod4(y + 1), zz)
        recv(("wy", -1, i))
        if i % 2 == 0:
            send(left, left, "wy", "wy far", yp)
        send(left, left, "wk", "wk", sib)
        recv(("wy", 1, i))
        if i % 2 == 1:
            send(right, right, "wy", "wy far", ym)
        send(right, right, "wk", "wk", sib)

    for a in range(2):
        kept[a].wait()
    recv("half")
    arrive(0)
    rest_x(0)
    w_in(0)
    arrive(1)
    rest_x(1)
    across(0)
    rest_x(2)
    rest_z(0)
    w_in(1)
    w_in(2)
    arrive(2)
    w_in(3)
    w_ring(0)
    across(1)
    rest_z(1)
    arrive(3)
    w_ring(1)
    across(2)
    w_ring(2)
    arrive(4)
    rest_z(2)
    w_ring(3)
    across(3)
    rest_z(3)
    recv("wy far")
    far = W.at[k, mod4(y + 2)]
    send(far, far, "wk", "wk", sib)
    across(4)
    recv("wk")

    def hidden_term(a, rel):
        blk = mod4(x + rel)
        term = lax.dot_general(
            W[a, blk], X[a, blk], (((0,), (0,)), ((), ())), preferred_element_type=F32
        )
        if rel == 0:
            H[a] = term
        else:
            H[a] += term

    for rel in (0, -1, 1):
        hidden_term(0, rel)
    recv(("rest", 4))
    for rel in (0, -1, 1):
        hidden_term(1, rel)
    recv("far")
    for a in range(2):
        hidden_term(a, 2)

    @pl.loop(0, 6)
    def _(i):
        rows = pl.ds(pl.multiple_of(i * 64, 64), 64)
        active, slope = gelu_pair(H[0, rows, :])
        hb[0, rows, :] = (H[1, rows, :] * slope).astype(BF16)
        hb[1, rows, :] = active.astype(BF16)

    def rows_of(start, size, align):
        return pl.ds(pl.multiple_of(start, align), size)

    def ig_block(rel):
        for i in range(3):
            rows = slice(i * 256, (i + 1) * 256)
            value = jnp.dot(W[0, mod4(x + rel), rows, :], hb[0], preferred_element_type=F32)
            if rel != 0:
                igb[rel % 4, rows, :] = value.astype(BF16)
            if rel != 2:
                igf[rel % 4, rows, :] = value

    def ig_spot(g, t):
        zt = mod8(z + (4 - g) * (1, -1)[t])
        whole = 0 < g < 4
        start = lax.rem(zt, 2) * 384 + (0 if whole else 192 * t)
        rows = rows_of(start, 384 if whole else 192, 192)
        return rows, rows_of(lax.div(zt, 2) * 128, 128, 128)

    def height(g):
        return slice(0, 384 if 0 < g < 4 else 192)

    def ig_s1(g):
        for t in range(2):
            send(
                igb.at[(2, *ig_spot(g, t))], igr.at[0, g, t, height(g)],
                "ig", ("ig", 0, g), (xp, xm)[t],
            )

    def ig_s2(g):
        for t in range(2):
            send(
                igb.at[((3, 1)[t], *ig_spot(g, t))], igr.at[1, g, t, height(g)],
                "ig", ("ig", 1, g), (xm, xp)[t],
            )

    def ig_got(stage, g, t):
        return igr[stage, g, t, height(g), :].astype(F32)

    def ig_s3(g):
        recv(("ig", 0, g))
        for t in range(2):
            value = igf[((1, 3)[t], *ig_spot(g, t))] + ig_got(0, g, t)
            igs[g, t, height(g), :] = value.astype(BF16)
            send(
                igs.at[g, t, height(g)], igr.at[2, g, t, height(g)],
                "ig", ("ig", 1, g), (xp, xm)[t],
            )

    def zc_got(g, t):
        return zr[g, t, height(g), :].astype(F32)

    def ig_s4(g):
        recv(("ig", 1, g))
        if 0 < g < 4:
            recv(("zc", g - 1))
        for t in range(2):
            value = igf[(0, *ig_spot(g, t))] + ig_got(1, g, t) + ig_got(2, g, t)
            if g == 4:
                own_sum[192 * t : 192 * (t + 1), :] = value
                continue
            if g > 1:
                value = value + zc_got(g - 1, t)
            zs[g, t, height(g), :] = value.astype(BF16)
            if g == 1:
                part_rows = slice(192 * t, 192 * (t + 1))
                summed = value[part_rows] + zc_got(0, t)
                zs[g, t, part_rows, :] = summed.astype(BF16)
            send(
                zs.at[g, t, height(g)], zr.at[g, t, height(g)],
                "zc", ("zc", g), (zp, zm)[t],
            )

    def dw_block(a, rel, rows):
        return lax.dot_general(
            X[a, mod4(y + rel), rows, :], hb[a], (((1,), (1,)), ((), ())),
            preferred_element_type=F32,
        )

    def dw_other(rel):
        for i in range(2):
            rows = slice(i * 384, (i + 1) * 384)
            ds[rel % 4, rows, :] = dw_block(o, rel, rows).astype(BF16)
            send(ds.at[rel % 4, rows, :], dr.at[rel % 4, rows, :], "dk", ("dk", rel), sib)

    def dw_own(rel):
        for i in range(2):
            rows = slice(i * 384, (i + 1) * 384)
            df[rel % 4, rows, :] = dw_block(k, rel, rows)

    def dw_sum(rel):
        recv(("dk", rel))

    def dw_value(rel, q, t):
        rows = slice(384 * t + 96 * q, 384 * t + 96 * (q + 1))
        return df[rel % 4, rows, :] + dr[rel % 4, rows, :].astype(F32)

    def dw_send(stage, q, t, value, device):
        dws[stage, q, t] = value.astype(BF16)
        send(dws.at[stage, q, t], dwr.at[stage, q, t], "dw", ("dw", min(stage, 1), q), device)

    def dw_got(stage, q, t):
        return dwr[stage, q, t].astype(F32)

    def dw_s1(q):
        for t in range(2):
            dw_send(0, q, t, dw_value(2, q, t), (yp, ym)[t])

    def dw_s2(q):
        for t in range(2):
            dw_send(1, q, t, dw_value((-1, 1)[t], q, t), (ym, yp)[t])

    def dw_s3(q):
        recv(("dw", 0, q))
        for t in range(2):
            dw_send(2, q, t, dw_value((1, -1)[t], q, t) + dw_got(0, q, t), (yp, ym)[t])

    d_at = recv_no("dl")

    def dw_place(a, h, q):
        return dw_out.at[
            a, 96 * (q % 2) : 96 * (q % 2 + 1), pl.ds(pl.multiple_of(h * 384, 128), 384)
        ]

    def dw_s4(q):
        recv(("dw", 1, q))
        for t in range(2):
            value = dw_value(0, q, t) + dw_got(1, q, t) + dw_got(2, q, t)
            dwl[q, t] = value.astype(BF16)
            zf = 2 * t + q // 2
            half = lax.rem(zh, 2)
            send_unless(
                jnp.logical_and(zf == zh, lax.div(zh, 2) == k),
                dwl.at[q, t],
                dw_place(k, half, q),
                "dl",
                dev(zz=2 * zf + zl, core=lax.div(zh, 2)),
                d_at,
            )

    ig_block(2)
    ig_s1(0)
    ig_s1(1)
    dw_other(2)
    ig_block(1)
    ig_block(-1)
    ig_s2(0)
    ig_s2(1)
    dw_own(2)
    dw_other(1)
    dw_other(-1)
    dw_sum(2)
    dw_s1(0)
    dw_s1(1)
    dw_own(1)
    dw_own(-1)
    dw_sum(1)
    dw_sum(-1)
    dw_s2(0)
    dw_s2(1)
    ig_block(0)
    dw_other(0)
    dw_own(0)
    dw_sum(0)
    ig_s3(0)
    ig_s1(2)
    ig_s2(2)
    dw_s3(0)
    dw_s1(2)
    dw_s2(2)
    ig_s3(1)
    ig_s1(3)
    ig_s2(3)
    ig_s4(0)
    dw_s3(1)
    dw_s1(3)
    dw_s2(3)
    dw_s4(0)
    ig_s3(2)
    ig_s1(4)
    ig_s2(4)
    ig_s4(1)
    dw_s3(2)
    dw_s4(1)
    ig_s3(3)
    ig_s4(2)
    dw_s3(3)
    dw_s4(2)
    ig_s3(4)
    ig_s4(3)
    dw_s4(3)
    ig_s4(4)

    recv(("zc", 3))
    last[...] = (own_sum[...] + zc_got(3, 0) + zc_got(3, 1)).astype(BF16)
    half = lambda core: last.at[pl.ds(pl.multiple_of(core * 192, 192), 192), :]
    send(half(o), ig_out.at[:, mine], "last", "last", sib)
    copy = pltpu.make_async_copy(half(k), ig_out.at[:, mine], local_sems.at[2])
    copy.start()
    copy.wait()
    recv("last")
    dummy(8 * BLOCK // 2, recv_at=d_at).wait_recv()

    for group, size in send_no.bytes.items():
        dummy(size, send_at=send_no(group)).wait_send()
    some_own = lax.div(zh, 2) == k

    @pl.when(some_own)
    def _():
        dummy(3 * BLOCK, send_at=send_no("w")).wait_send()
        dummy(6 * BLOCK // 2, send_at=send_no("dl")).wait_send()

    @pl.when(jnp.logical_not(some_own))
    def _():
        dummy(4 * BLOCK, send_at=send_no("w")).wait_send()
        dummy(8 * BLOCK // 2, send_at=send_no("dl")).wait_send()

    assert send_no.count <= SENDS and recv_no.count <= RECVS


def body(tokens, out_grad, w_up, w_down):
    any_ = pl.BlockSpec(memory_space=pl.ANY)
    dw, ig = pl.pallas_call(
        kernel,
        out_shape=(
            jax.ShapeDtypeStruct((2, 192, 768), BF16),
            jax.ShapeDtypeStruct((192, 256), BF16),
        ),
        in_specs=[any_] * 4,
        out_specs=(any_, any_),
        scratch_shapes=[
            pltpu.VMEM((2, 4, 768, 512), BF16),
            pltpu.VMEM((2, 4, 768, 384), BF16),
            pltpu.VMEM((2, 384, 512), F32),
            pltpu.VMEM((2, 384, 512), BF16),
            pltpu.VMEM((4, 768, 512), BF16),
            pltpu.VMEM((4, 768, 512), F32),
            pltpu.VMEM((5, 2, 384, 128), BF16),
            pltpu.VMEM((3, 5, 2, 384, 128), BF16),
            pltpu.VMEM((4, 2, 384, 128), BF16),
            pltpu.VMEM((4, 2, 384, 128), BF16),
            pltpu.VMEM((384, 128), F32),
            pltpu.VMEM((384, 128), BF16),
            pltpu.VMEM((4, 768, 384), BF16),
            pltpu.VMEM((4, 768, 384), BF16),
            pltpu.VMEM((4, 768, 384), F32),
            pltpu.VMEM((3, 4, 2, 96, 384), BF16),
            pltpu.VMEM((3, 4, 2, 96, 384), BF16),
            pltpu.VMEM((4, 2, 96, 384), BF16),
            pltpu.SemaphoreType.DMA((SENDS,)),
            pltpu.SemaphoreType.DMA((RECVS,)),
            pltpu.SemaphoreType.DMA((4,)),
        ],
        compiler_params=pltpu.CompilerParams(
            collective_id=0, has_side_effects=True, vmem_limit_bytes=58 * 2**20
        ),
        cost_estimate=pl.CostEstimate(
            flops=6 * 10**9, bytes_accessed=4 * 10**6, transcendentals=2 * 10**5
        ),
        name="ffn_backward",
    )(tokens.T, out_grad.T, w_up, w_down)
    factor = 1.0 / math.sqrt(tokens.shape[0] * lax.axis_size("row"))
    return (ig.T, dw[0].astype(F32) * factor, dw[1].astype(F32) * factor)


def solution(mesh):
    return jax.shard_map(
        body,
        mesh=mesh,
        in_specs=(P("row", "col"), P("row", "col"), P("row", "col"), P("row", "col")),
        out_specs=(P("row", "col"), P("row", "col"), P("row", "col")),
        check_vma=False,
    )
```

time: 125 us -> 111 us (0.89)
  Pallas kernels: 122 us -> 107 us
    pallas_call x1, Pallas kernels: 122 us -> 107 us  [body(): pl.pallas_call(kernel, out_shape=(jax.ShapeDtypeStruct((2, 192, 768), BF1...]
where the time goes in v3:
time: 111 us
  Pallas kernels  107 us (96%)
  other arithmetic  2.17 us (2%)
    pallas_call x1, Pallas kernels, body(): pl.pallas_call(kernel, out_shape=(jax.ShapeDtypeStruct((2, 192, 768), BF1...  107 us

profile of v3, /device:TPU:65, one launch (start us, length us, event | category | flops | bytes accessed | tf_op | source)
XLA Modules:
  0.0 110.7 jit_solution(16723121039522838985)
XLA Ops:
  0.6 107.3 %ffn_backward.1 = (bf16[2,192,768]{2,1,0:T(8,128)(2,1)}, bf16[192,256]{1,0:T(8,128)(2,1)}) custom-call(bf16[192,256]{1,0:T(8,128)(2,1)} %bitcast.8, bf16[192,256]{1,0:T(8,128)(2,1)} %bitcast.9, bf16[192,768]{1,0:T(8,128)(2,1)} %wu.1, bf16[192,768]{1,0:T(8,128)(2,1)} %wd.1), custom_call_target="tpu_custom_call" | custom-call | flops 6000000000 | bytes 4000000 | tf_op jit(solution)/shard_map/ffn_backward/pallas_call | solution.py:559
  107.9 0.0 copy-start
  107.9 2.2 %multiply_bitcast_fusion = (f32[192,768]{1,0:T(8,128)}, f32[192,768]{1,0:T(8,128)}) fusion(bf16[2,192,768]{2,1,0:T(8,128)(2,1)} %get-tuple-element.6), kind=kLoop, calls=%fused_computation | loop fusion | flops 589824 | bytes 1769472 | tf_op jit(solution)/shard_map/mul | solution.py:599
  110.1 0.0 copy-done
  110.1 0.6 copy.8
Async XLA Ops:
  107.9 2.2 %copy-start = (bf16[192,256]{1,0:T(8,128)(2,1)S(1)}, bf16[192,256]{1,0:T(8,128)(2,1)}, u32[]{:S(2)}) copy-start(bf16[192,256]{1,0:T(8,128)(2,1)} %get-tuple-element.5) | copy-start | bytes 294916

commit v4 on v3

--- a/solution.py
+++ b/solution.py
@@ -41,9 +41,10 @@
         return self(key)
 
 
-SENDS = 13
-RECVS = 76
+SENDS = 14
+RECVS = 86
 BLOCK = 192 * 384 * 2
+CUT = 98304
 
 
 def kernel(
@@ -88,10 +89,8 @@
         copy.start()
 
     barrier = pltpu.get_barrier_semaphore()
-    partners = [sib, xp, xm, yp, ym, zp, zm]
-    for rel in (2, 4, 6):
-        for core in (k, o):
-            partners.append(dev(zz=mod8(z + rel), core=core))
+    partners = [dev(zz=mod8(z + rel), core=core) for rel in (4, 2, 6) for core in (k, o)]
+    partners += [xp, xm, yp, ym, zp, zm, sib]
     for partner in partners:
         pl.semaphore_signal(barrier, inc=1, device_id=partner, device_id_type=MESH)
     pl.semaphore_wait(barrier, len(partners))
@@ -102,16 +101,13 @@
         return math.prod(ref.shape) * 2
 
     def view(size):
-        for lead in (1, 2, 3, 4, 6, 8):
-            rows, rest = divmod(size, lead * 1024)
-            if rest == 0 and rows <= 768 and rows % 16 == 0:
-                if lead < 5:
-                    return X.at[0, :lead, :rows, :]
-                return X.at[:, : lead // 2, :rows, :]
-        for rows in range(768, 0, -16):
-            for lead in (1, 2, 3, 4):
-                if size == lead * rows * 256:
-                    return X.at[0, :lead, :rows, :128]
+        for lanes in (512, 384, 256, 128):
+            for lead in (1, 2, 3, 4, 6, 8):
+                rows, rest = divmod(size, lead * lanes * 2)
+                if rest == 0 and rows <= 768 and rows % 16 == 0:
+                    if lead < 5:
+                        return X.at[0, :lead, :rows, :lanes]
+                    return X.at[:, : lead // 2, :rows, :lanes]
         raise ValueError(size)
 
     def dummy(size, send_at=0, recv_at=0):
@@ -124,35 +120,42 @@
             device_id_type=MESH,
         )
 
+    def cuts(ref):
+        if len(ref.shape) == 3:
+            return [piece for n in range(ref.shape[0]) for piece in cuts(ref.at[n])]
+        rows, lanes = ref.shape
+        most = max(16, CUT // (lanes * 2) // 16 * 16)
+        count = -(-rows // most)
+        size = -(-rows // count // 16) * 16
+        return [ref.at[pl.ds(n, min(size, rows - n)), :] for n in range(0, rows, size)]
+
+    def copies(src, dst, send_at, recv_at, device):
+        return [
+            pltpu.make_async_remote_copy(
+                src_ref=one,
+                dst_ref=other_,
+                send_sem=send_sems.at[send_at],
+                recv_sem=recv_sems.at[recv_at],
+                device_id=device,
+                device_id_type=MESH,
+            )
+            for one, other_ in zip(cuts(src), cuts(dst))
+        ]
+
     def send(src, dst, group, key, device):
         size = size_of(src)
-        pltpu.make_async_remote_copy(
-            src_ref=src,
-            dst_ref=dst,
-            send_sem=send_sems.at[send_no.add(group, size)],
-            recv_sem=recv_sems.at[recv_no.add(key, size)],
-            device_id=device,
-            device_id_type=MESH,
-        ).start()
+        for copy in copies(src, dst, send_no.add(group, size), recv_no.add(key, size), device):
+            copy.start()
 
     def send_unless(own, src, dst, group, device, recv_at):
-        copy = pltpu.make_async_remote_copy(
-            src_ref=src,
-            dst_ref=dst,
-            send_sem=send_sems.at[send_no(group)],
-            recv_sem=recv_sems.at[recv_at],
-            device_id=device,
-            device_id_type=MESH,
-        )
-        local = pltpu.make_async_copy(src, dst, recv_sems.at[recv_at])
-
         @pl.when(own)
         def _():
-            local.start()
+            pltpu.make_async_copy(src, dst, recv_sems.at[recv_at]).start()
 
         @pl.when(jnp.logical_not(own))
         def _():
-            copy.start()
+            for copy in copies(src, dst, send_no(group), recv_at, device):
+                copy.start()
 
     def recv(key):
         dummy(recv_no.bytes[key], recv_at=recv_no(key)).wait_recv()
@@ -162,22 +165,19 @@
 
     w_base = recv_no("w", 4)
 
-    def w_out(a):
-        for h in range(2):
-            zt = 2 * k + h
-            send_unless(
-                jnp.logical_and(zt == zh, k == a),
-                (wu, wd)[a].at[:, h * 384 : (h + 1) * 384],
-                w_rows(a, y, zh),
-                "w",
-                dev(zz=2 * zt + zl, core=a),
-                w_base + zh,
-            )
+    def w_out(a, h):
+        zt = 2 * k + h
+        send_unless(
+            jnp.logical_and(zt == zh, k == a),
+            (wu, wd)[a].at[:, h * 384 : (h + 1) * 384],
+            w_rows(a, y, zh),
+            "w",
+            dev(zz=2 * zt + zl, core=a),
+            w_base + zh,
+        )
 
     for a, src in enumerate((tok, og)):
         send(src.at[:, other], part(a, k), "half", "half", sib)
-    w_out(0)
-    w_out(1)
 
     def lanes_of(zz):
         return pl.ds(pl.multiple_of(lax.div(zz, 2) * 128, 128), 128)
@@ -200,23 +200,35 @@
 
     steps = [[0], [-1, 1], [-2, 2], [-3, 3], [4]]
 
+    def near(rel, n, block):
+        send(block, block, "x", ("x", -1, rel) if n == rel % 2 else "near", xp)
+        send(block, block, "x", ("x", 1, rel) if n != rel % 2 else "near", xm)
+
+    def first():
+        block = part(0, k)
+        for device, key in ((xp, -1), (xm, 1)):
+            send(tok.at[:, mine], block, "x", ("x", key, 0) if key == -1 else "near", device)
+        send(tok.at[:, mine], block, "z", ("z", -1, 0), zp)
+        send(tok.at[:, mine], block, "z", ("z", 1, 0), zm)
+
     def arrive(step):
         for rel in steps[step]:
             blocks = [tok_shard(x, mod8(z + rel)), og_shard(x, mod8(z + rel))]
-            if step > 0:
-                recv(("z", rel))
+            if step == 0:
+                blocks[0] = part(0, o)
             for n, block in enumerate(blocks):
+                if step > 0:
+                    recv(("z", rel, n))
                 if step < 3 and rel <= 0:
-                    send(block, block, "z", ("z", rel - 1), zp)
+                    send(block, block, "z", ("z", rel - 1, n), zp)
                 if step < 3 and rel >= 0:
-                    send(block, block, "z", ("z", rel + 1), zm)
+                    send(block, block, "z", ("z", rel + 1, n), zm)
                 if rel == -3 and n == 0:
-                    send(block, block, "z", ("z", 4), zp)
+                    send(block, block, "z", ("z", 4, n), zp)
                 if rel == 3 and n == 1:
-                    send(block, block, "z", ("z", 4), zm)
-            for block in blocks:
-                send(block, block, "x", ("x", -1, rel), xp)
-                send(block, block, "x", ("x", 1, rel), xm)
+                    send(block, block, "z", ("z", 4, n), zm)
+            for n, block in enumerate(blocks):
+                near(rel, n, block)
 
     def across(step):
         for rel in steps[step]:
@@ -231,13 +243,13 @@
     def rest_x(step):
         if step == 0:
             block = rest_shard(x, 0, 192)
-            send(block, block, "rest", "rest near", xp)
-            send(block, block, "rest", "rest near", xm)
+            send(block, block, "rest x", "rest near", xp)
+            send(block, block, "rest x", "rest near", xm)
         if step == 1:
             recv("rest near")
             left, right = rest_shard(mod4(x - 1), 0, 96), rest_shard(mod4(x + 1), 96, 96)
-            send(left, left, "rest", "rest far", xp)
-            send(right, right, "rest", "rest far", xm)
+            send(left, left, "rest x", "rest far", xp)
+            send(right, right, "rest x", "rest far", xm)
         if step == 2:
             recv("rest far")
 
@@ -275,33 +287,38 @@
             send(right, right, "wy", "wy far", ym)
         send(right, right, "wk", "wk", sib)
 
+    first()
+    w_out(0, 0)
     for a in range(2):
         kept[a].wait()
     recv("half")
     arrive(0)
     rest_x(0)
-    w_in(0)
+    w_out(0, 1)
     arrive(1)
     rest_x(1)
+    w_out(1, 0)
+    w_out(1, 1)
+    w_in(0)
     across(0)
-    rest_x(2)
-    rest_z(0)
     w_in(1)
     w_in(2)
     arrive(2)
     w_in(3)
+    rest_x(2)
+    rest_z(0)
+    across(1)
     w_ring(0)
-    across(1)
-    rest_z(1)
     arrive(3)
     w_ring(1)
-    across(2)
+    rest_z(1)
     w_ring(2)
     arrive(4)
     rest_z(2)
+    across(2)
     w_ring(3)
+    rest_z(3)
     across(3)
-    rest_z(3)
     recv("wy far")
     far = W.at[k, mod4(y + 2)]
     send(far, far, "wk", "wk", sib)
@@ -318,6 +335,7 @@
         else:
             H[a] += term
 
+    recv("near")
     for rel in (0, -1, 1):
         hidden_term(0, rel)
     recv(("rest", 4))
@@ -454,9 +472,8 @@
     d_at = recv_no("dl")
 
     def dw_place(a, h, q):
-        return dw_out.at[
-            a, 96 * (q % 2) : 96 * (q % 2 + 1), pl.ds(pl.multiple_of(h * 384, 128), 384)
-        ]
+        start = pl.multiple_of(a * 768 + h * 384, 384)
+        return dw_out.at[96 * (q % 2) : 96 * (q % 2 + 1), pl.ds(start, 384)]
 
     def dw_s4(q):
         recv(("dw", 1, q))
@@ -474,58 +491,58 @@
                 d_at,
             )
 
+    dw_other(2)
     ig_block(2)
     ig_s1(0)
-    ig_s1(1)
-    dw_other(2)
+    dw_own(2)
     ig_block(1)
     ig_block(-1)
     ig_s2(0)
-    ig_s2(1)
-    dw_own(2)
-    dw_other(1)
-    dw_other(-1)
+    ig_s1(1)
     dw_sum(2)
     dw_s1(0)
     dw_s1(1)
+    dw_other(1)
+    dw_other(-1)
+    dw_other(0)
     dw_own(1)
     dw_own(-1)
+    dw_own(0)
+    ig_s3(0)
+    ig_s2(1)
+    ig_block(0)
     dw_sum(1)
     dw_sum(-1)
     dw_s2(0)
+    dw_sum(0)
+    ig_s1(2)
+    dw_s3(0)
     dw_s2(1)
-    ig_block(0)
-    dw_other(0)
-    dw_own(0)
-    dw_sum(0)
-    ig_s3(0)
-    ig_s1(2)
+    ig_s3(1)
     ig_s2(2)
-    dw_s3(0)
+    ig_s4(0)
     dw_s1(2)
+    ig_s1(3)
+    dw_s3(1)
     dw_s2(2)
-    ig_s3(1)
-    ig_s1(3)
-    ig_s2(3)
-    ig_s4(0)
-    dw_s3(1)
-    dw_s1(3)
-    dw_s2(3)
     dw_s4(0)
     ig_s3(2)
+    ig_s2(3)
+    ig_s4(1)
+    dw_s1(3)
     ig_s1(4)
-    ig_s2(4)
-    ig_s4(1)
     dw_s3(2)
+    dw_s2(3)
     dw_s4(1)
     ig_s3(3)
+    ig_s2(4)
     ig_s4(2)
     dw_s3(3)
     dw_s4(2)
     ig_s3(4)
     ig_s4(3)
+    ig_s4(4)
     dw_s4(3)
-    ig_s4(4)
 
     recv(("zc", 3))
     last[...] = (own_sum[...] + zc_got(3, 0) + zc_got(3, 1)).astype(BF16)
@@ -559,7 +576,7 @@
     dw, ig = pl.pallas_call(
         kernel,
         out_shape=(
-            jax.ShapeDtypeStruct((2, 192, 768), BF16),
+            jax.ShapeDtypeStruct((192, 1536), BF16),
             jax.ShapeDtypeStruct((192, 256), BF16),
         ),
         in_specs=[any_] * 4,
@@ -596,7 +613,7 @@
         name="ffn_backward",
     )(tokens.T, out_grad.T, w_up, w_down)
     factor = 1.0 / math.sqrt(tokens.shape[0] * lax.axis_size("row"))
-    return (ig.T, dw[0].astype(F32) * factor, dw[1].astype(F32) * factor)
+    return (ig.T, dw[:, :768].astype(F32) * factor, dw[:, 768:].astype(F32) * factor)
 
 
 def solution(mesh):

time: 111 us -> 103 us (0.928)
  Pallas kernels: 107 us -> 99.2 us
    pallas_call x1, Pallas kernels: 107 us -> 99.2 us  [body(): pl.pallas_call(kernel, out_shape=(jax.ShapeDtypeStruct((192, 1536), BF16)...]
where the time goes in v4:
time: 103 us
  Pallas kernels  99.2 us (96%)
  other arithmetic  2.17 us (2%)
    pallas_call x1, Pallas kernels, body(): pl.pallas_call(kernel, out_shape=(jax.ShapeDtypeStruct((192, 1536), BF16)...  99.2 us
    mul x1, other arithmetic, body(): dw[:, 768:].astype(F32) * factor  2.17 us

profile of v4, /device:TPU:65, one launch (start us, length us, event | category | flops | bytes accessed | tf_op | source)
XLA Modules:
  0.0 102.7 jit_solution(11632371383246165916)
XLA Ops:
  0.6 99.2 %ffn_backward.1 = (bf16[192,1536]{1,0:T(8,128)(2,1)}, bf16[192,256]{1,0:T(8,128)(2,1)}) custom-call(bf16[192,256]{1,0:T(8,128)(2,1)} %bitcast.4, bf16[192,256]{1,0:T(8,128)(2,1)} %bitcast.5, bf16[192,768]{1,0:T(8,128)(2,1)} %wu.1, bf16[192,768]{1,0:T(8,128)(2,1)} %wd.1), custom_call_target="tpu_custom_call" | custom-call | flops 6000000000 | bytes 4000000 | tf_op jit(solution)/shard_map/ffn_backward/pallas_call | solution.py:576
  99.9 0.0 copy-start
  99.9 2.2 %convert_multiply_fusion = (f32[192,768]{1,0:T(8,128)}, f32[192,768]{1,0:T(8,128)}) fusion(bf16[192,1536]{1,0:T(8,128)(2,1)} %get-tuple-element.6), kind=kLoop, calls=%fused_computation | loop fusion | flops 589824 | bytes 1769472 | tf_op jit(solution)/shard_map/mul | solution.py:616
  102.1 0.0 copy-done
  102.1 0.6 copy.8
Async XLA Ops:
  99.9 2.2 %copy-start = (bf16[192,256]{1,0:T(8,128)(2,1)S(1)}, bf16[192,256]{1,0:T(8,128)(2,1)}, u32[]{:S(2)}) copy-start(bf16[192,256]{1,0:T(8,128)(2,1)} %get-tuple-element.5) | copy-start | bytes 294916

commit v5 on v4

--- a/solution.py
+++ b/solution.py
@@ -292,13 +292,13 @@
     for a in range(2):
         kept[a].wait()
     recv("half")
+    rest_x(0)
     arrive(0)
-    rest_x(0)
     w_out(0, 1)
     arrive(1)
-    rest_x(1)
     w_out(1, 0)
     w_out(1, 1)
+    rest_x(1)
     w_in(0)
     across(0)
     w_in(1)

time: 103 us -> 102 us (level)
  no operation moved by 1% of the time
where the time goes in v5:
time: 102 us
  Pallas kernels  98.9 us (97%)
  other arithmetic  2.17 us (2%)
    pallas_call x1, Pallas kernels, body(): pl.pallas_call(kernel, out_shape=(jax.ShapeDtypeStruct((192, 1536), BF16)...  98.9 us
    mul x1, other arithmetic, body(): dw[:, 768:].astype(F32) * factor  2.17 us

profile of v5, /device:TPU:65, one launch (start us, length us, event | category | flops | bytes accessed | tf_op | source)
XLA Modules:
  0.0 102.4 jit_solution(9347628688870240601)
XLA Ops:
  0.6 98.9 %ffn_backward.1 = (bf16[192,1536]{1,0:T(8,128)(2,1)}, bf16[192,256]{1,0:T(8,128)(2,1)}) custom-call(bf16[192,256]{1,0:T(8,128)(2,1)} %bitcast.4, bf16[192,256]{1,0:T(8,128)(2,1)} %bitcast.5, bf16[192,768]{1,0:T(8,128)(2,1)} %wu.1, bf16[192,768]{1,0:T(8,128)(2,1)} %wd.1), custom_call_target="tpu_custom_call" | custom-call | flops 6000000000 | bytes 4000000 | tf_op jit(solution)/shard_map/ffn_backward/pallas_call | solution.py:576
  99.6 0.0 copy-start
  99.6 2.2 %convert_multiply_fusion = (f32[192,768]{1,0:T(8,128)}, f32[192,768]{1,0:T(8,128)}) fusion(bf16[192,1536]{1,0:T(8,128)(2,1)} %get-tuple-element.6), kind=kLoop, calls=%fused_computation | loop fusion | flops 589824 | bytes 1769472 | tf_op jit(solution)/shard_map/mul | solution.py:616
  101.7 0.0 copy-done
  101.7 0.6 copy.8
Async XLA Ops:
  99.6 2.2 %copy-start = (bf16[192,256]{1,0:T(8,128)(2,1)S(1)}, bf16[192,256]{1,0:T(8,128)(2,1)}, u32[]{:S(2)}) copy-start(bf16[192,256]{1,0:T(8,128)(2,1)} %get-tuple-element.5) | copy-start | bytes 294916
